TPU v7x, 32 devices: a whole 2x2x4 slice. The times are simulated.
32 devices in a mesh: dp: 4 (over z), owner: 8 (over y, x, core).
Axes of the slice: x: 2, y: 2, z: 4, core: 2. Of those that a mesh axis runs over, the one named last changes fastest.
Arguments:
- tokens: bfloat16 [4096, 8192], P(('dp', 'owner')), may hold values from -6 to 6
- residual: bfloat16 [4096, 8192], P(('dp', 'owner')), may hold values from -6 to 6
- token_adapter_index: int32 [4096, 1], P(('dp', 'owner')), may hold values from 0 to 7; in each aligned block of 128 rows (0 to 127, 128 to 255, ...) at most 24 rows name the same one
- adapter_down_weight: bfloat16 [8, 64, 8192], P('owner', None, 'dp'), may hold values from -0.0625 to 0.0625
- adapter_up_weight: bfloat16 [8, 64, 8192], P('owner', None, 'dp'), may hold values from -0.75 to 0.75
- down_moment_first: bfloat16 [8, 64, 8192], P('owner', None, 'dp'), may hold values from -135 to 135
- down_moment_second: bfloat16 [8, 64, 8192], P('owner', None, 'dp'), may hold values from 204 to 6144
- up_moment_first: bfloat16 [8, 64, 8192], P('owner', None, 'dp'), may hold values from -13.5625 to 13.5625
- up_moment_second: bfloat16 [8, 64, 8192], P('owner', None, 'dp'), may hold values from 1.53125 to 51
Outputs:
- down_update: float32 [8, 64, 8192], P('owner', None, 'dp')
- up_update: float32 [8, 64, 8192], P('owner', None, 'dp')
- token_loss: float32 [4096], P(('dp', 'owner'))
Inputs may be any that keep to these rules, and one draw needn't show every extreme that they name: `token_adapter_index`: of the 128 rows of one device, at most 24 name one adapter, and in some devices one adapter is named by exactly 24.
All inputs are finite; a program needn't handle non-finite values.
Results may differ from a plain program's by a relative error of at most 0.0091.
Values may be sent and summed in bfloat16 or wider, within the bound.
A program may use at most 128 MiB of HBM per device.

v0:
```python
import jax
import jax.numpy as jnp
from jax import lax
from jax.sharding import PartitionSpec as P

adapter_scale = 0.5
adam_eps = 1e-08


def adam_update(grad, first, second):
    first_new = 0.9 * first.astype(jnp.float32) + 0.1 * grad
    second_new = 0.95 * second.astype(jnp.float32) + 0.05 * grad * grad
    return first_new / (jnp.sqrt(second_new) + adam_eps)


def body(
    tokens,
    residual,
    token_adapter_index,
    adapter_down_weight,
    adapter_up_weight,
    down_moment_first,
    down_moment_second,
    up_moment_first,
    up_moment_second,
):
    owner_index = lax.axis_size("owner")
    tok_rows = tokens.shape[0]
    model_width_value = tokens.shape[1]
    column_span = adapter_down_weight.shape[2]
    slot_capacity = max(2, 3 * tok_rows // (2 * owner_index))
    route_ids = token_adapter_index[:, 0]
    member = (route_ids[:, None] == jnp.arange(owner_index, dtype=jnp.int32)[None, :]).astype(
        jnp.int32
    )
    before = jnp.cumsum(member, axis=0) - member
    within = jnp.sum(before * member, axis=1)
    target = route_ids * slot_capacity + within
    dispatch = (
        jnp.arange(owner_index * slot_capacity, dtype=jnp.int32)[:, None] == target[None, :]
    ).astype(jnp.bfloat16)

    def placed_rows(row_block):
        return jnp.dot(dispatch, row_block, preferred_element_type=jnp.float32).astype(jnp.bfloat16)

    down_full, up_weight_whole = (
        lax.all_gather(adapter_down_weight, "dp", axis=2, tiled=True),
        lax.all_gather(adapter_up_weight, "dp", axis=2, tiled=True),
    )
    down_full = down_full[0]
    up_weight_whole = up_weight_whole[0]

    def spread(row_block):
        return placed_rows(row_block).reshape(owner_index, slot_capacity, model_width_value)

    arrived = lax.all_to_all(
        spread(tokens), "owner", split_axis=0, concat_axis=0, tiled=True
    ).reshape(owner_index * slot_capacity, model_width_value)
    hidden_state = lax.dot_general(
        arrived, down_full, (((1,), (1,)), ((), ())), preferred_element_type=jnp.float32
    ).astype(jnp.bfloat16)
    adapter_output = (
        adapter_scale * jnp.dot(hidden_state, up_weight_whole, preferred_element_type=jnp.float32)
    ).astype(jnp.bfloat16)
    hidden_state, adapter_output = (hidden_state, adapter_output)
    returned = lax.all_to_all(
        adapter_output.reshape(owner_index, slot_capacity, model_width_value),
        "owner",
        split_axis=0,
        concat_axis=0,
        tiled=True,
    )
    returned = returned.reshape(owner_index * slot_capacity, model_width_value)
    adapter_home_index = lax.dot_general(
        dispatch, returned, (((0,), (0,)), ((), ())), preferred_element_type=jnp.float32
    )
    shifted_index = residual.astype(jnp.float32) + adapter_home_index
    token_loss = jnp.mean(0.5 * shifted_index * shifted_index, axis=1)
    output_gradient = lax.all_to_all(
        spread(shifted_index.astype(jnp.bfloat16)), "owner", split_axis=0, concat_axis=0, tiled=True
    )
    output_gradient = output_gradient.reshape(owner_index * slot_capacity, model_width_value)
    up_gradient = adapter_scale * lax.dot_general(
        hidden_state, output_gradient, (((0,), (0,)), ((), ())), preferred_element_type=jnp.float32
    )
    hidden_gradient = (
        adapter_scale
        * lax.dot_general(
            output_gradient,
            up_weight_whole,
            (((1,), (1,)), ((), ())),
            preferred_element_type=jnp.float32,
        )
    ).astype(jnp.bfloat16)
    down_grad = lax.dot_general(
        hidden_gradient, arrived, (((0,), (0,)), ((), ())), preferred_element_type=jnp.float32
    )
    summed_down, summed_up = lax.psum((down_grad, up_gradient), "dp")
    offset = lax.axis_index("dp") * column_span
    down_share = lax.dynamic_slice_in_dim(summed_down, offset, column_span, 1)
    up_share = lax.dynamic_slice_in_dim(summed_up, offset, column_span, 1)
    down_update = adam_update(down_share, down_moment_first[0], down_moment_second[0])
    up_update = adam_update(up_share, up_moment_first[0], up_moment_second[0])
    return (down_update[None], up_update[None], token_loss)


def solution(mesh):
    return jax.shard_map(
        body,
        mesh=mesh,
        in_specs=(
            P(("dp", "owner"), None),
            P(("dp", "owner"), None),
            P(("dp", "owner"), None),
            P("owner", None, "dp"),
            P("owner", None, "dp"),
            P("owner", None, "dp"),
            P("owner", None, "dp"),
            P("owner", None, "dp"),
            P("owner", None, "dp"),
        ),
        out_specs=(P("owner", None, "dp"), P("owner", None, "dp"), P(("dp", "owner"))),
        check_vma=False,
    )
```

profile of v0, /device:TPU:9, one launch (start us, length us, event | category | flops | bytes accessed | tf_op | source)
XLA Modules:
  0.0 324.9 jit_solution(15100237552305673756)
XLA Ops:
  7.2 0.7 all-gather.3.cloned.1.call-update
  7.9 0.7 fusion.19
  8.7 0.2 reduce_window_sum.11
  8.8 0.8 select_reduce_fusion
  9.7 0.7 multiply_add_fusion
  10.3 2.6 convolution_convert_fusion.1
  13.0 5.0 %all-to-all-start = ((bf16[8,24,8192]{2,1,0:T(8,128)(2,1)}), bf16[8,24,8192]{2,1,0:T(8,128)(2,1)}, u32[]{:S(2)}, u32[]{:S(2)}) async-start(bf16[8,24,8192]{2,1,0:T(8,128)(2,1)} %bitcast.45), calls=%async_computation | async-start | bytes 6291456 | tf_op jit(solution)/shard_map/all_to_all | solution.py:56
  18.0 0.7 all-gather.5.cloned.1.call-update
  18.7 0.0 all-reduce.3.cloned.1.call-start
  18.8 19.7 %all-gather.3.cloned.1.call-done = bf16[1,64,8192]{2,1,0:T(8,128)(2,1)} async-done(((bf16[1,64,2048]{2,1,0:T(8,128)(2,1)}), bf16[1,64,8192]{2,1,0:T(8,128)(2,1)}) %all-gather.3.cloned.1.call-update) | async-done | bytes 1048592 | tf_op jit(solution)/shard_map/all_gather | solution.py:47
  38.5 13.9 %all-to-all-done = bf16[8,24,8192]{2,1,0:T(8,128)(2,1)} async-done(((bf16[8,24,8192]{2,1,0:T(8,128)(2,1)}), bf16[8,24,8192]{2,1,0:T(8,128)(2,1)}, u32[]{:S(2)}, u32[]{:S(2)}) %all-to-all-start) | async-done | bytes 3145760 | tf_op jit(solution)/shard_map/all_to_all | solution.py:56
  52.4 3.3 %convolution_convert_fusion.2 = bf16[192,64]{0,1:T(8,128)(2,1)S(1)} fusion(bf16[192,8192]{1,0:T(8,128)(2,1)} %bitcast.3, bf16[1,64,8192]{2,1,0:T(8,128)(2,1)} %all-gather.3.cloned.1.call-done), kind=kOutput, calls=%fused_computation.11 | convolution fusion | flops 201338880 | bytes 4218880 | tf_op jit(solution)/shard_map/dot_general | solution.py:59
  55.7 11.8 %all-gather.5.cloned.1.call-done = bf16[1,64,8192]{2,1,0:T(8,128)(2,1)} async-done(((bf16[1,64,2048]{2,1,0:T(8,128)(2,1)}), bf16[1,64,8192]{2,1,0:T(8,128)(2,1)}) %all-gather.5.cloned.1.call-update) | async-done | bytes 1048592 | tf_op jit(solution)/shard_map/all_gather | solution.py:48
  67.5 2.2 fusion
  69.7 41.0 %all_to_all.15 = bf16[8,24,8192]{2,1,0:T(8,128)(2,1)S(1)} all-to-all(bf16[8,24,8192]{2,1,0:T(8,128)(2,1)S(1)} %bitcast.44), channel_id=1, replica_groups=mesh['dp'=4,'owner'=8] {'owner'}, dimensions={0} | all-to-all | bytes 6291456 | tf_op jit(solution)/shard_map/all_to_all | solution.py:66
  110.7 1.4 fusion.1
  112.1 1.0 convolution_convert_fusion
  113.1 40.3 %all_to_all.16 = bf16[8,24,8192]{2,1,0:T(8,128)(2,1)S(1)} all-to-all(bf16[8,24,8192]{2,1,0:T(8,128)(2,1)S(1)} %bitcast.46), channel_id=1, replica_groups=mesh['dp'=4,'owner'=8] {'owner'}, dimensions={0} | all-to-all | bytes 6291456 | tf_op jit(solution)/shard_map/all_to_all | solution.py:79
  153.4 1.7 copy-done.1
  155.1 2.1 convolution_multiply_fusion.1
  157.1 6.5 %fusion.4 = f32[64,8192]{1,0:T(8,128)} fusion(bf16[192,8192]{1,0:T(8,128)(2,1)} %bitcast.3, bf16[192,8192]{1,0:T(8,128)(2,1)} %bitcast.43, bf16[1,64,8192]{2,1,0:T(8,128)(2,1)S(1)} %copy-done.2), kind=kOutput, calls=%fused_computation.12 | convolution fusion | flops 402677760 | bytes 9437184 | tf_op jit(solution)/shard_map/dot_general | solution.py:95
  163.7 0.5 broadcast_multiply_fusion
  164.2 151.3 %all-reduce.3.cloned.1.call-done = (f32[64,8192]{1,0:T(8,128)}, f32[64,8192]{1,0:T(8,128)}) async-done(((f32[64,8192]{1,0:T(8,128)}, f32[64,8192]{1,0:T(8,128)}), (f32[64,8192]{1,0:T(8,128)}, f32[64,8192]{1,0:T(8,128)})) %all-reduce.3.cloned.1.call-update) | async-done | bytes 4194320 | tf_op jit(solution)/shard_map/psum | solution.py:98
  315.6 2.8 fusion.13
  (18 shorter events, 0.1 us)
Async XLA Ops:
  7.2 3.2 copy-start
  7.2 31.3 %all-gather.3.cloned.1.call-start = ((), (), s32[]{:S(2)}) async-start(), calls=%async_computation.3 | async-start | bytes 1310720 | tf_op jit(solution)/shard_map/all_gather | solution.py:47
  13.0 39.4 %all-to-all-start = ((bf16[8,24,8192]{2,1,0:T(8,128)(2,1)}), bf16[8,24,8192]{2,1,0:T(8,128)(2,1)}, u32[]{:S(2)}, u32[]{:S(2)}) async-start(bf16[8,24,8192]{2,1,0:T(8,128)(2,1)} %bitcast.45), calls=%async_computation | async-start | bytes 6291456 | tf_op jit(solution)/shard_map/all_to_all | solution.py:56
  18.0 49.5 %all-gather.5.cloned.1.call-start = ((), (), s32[]{:S(2)}) async-start(), calls=%async_computation.4 | async-start | bytes 1310720 | tf_op jit(solution)/shard_map/all_gather | solution.py:48
  18.7 296.8 %all-reduce.3.cloned.1.call-start = ((), (), s32[]{:S(2)}) async-start(), calls=%async_computation.5 | async-start | bytes 8388608 | tf_op jit(solution)/shard_map/psum | solution.py:98
  69.7 41.0 %copy-start.7 = (bf16[128,8192]{1,0:T(8,128)(2,1)S(1)}, bf16[128,8192]{1,0:T(8,128)(2,1)}, u32[]{:S(2)}) copy-start(bf16[128,8192]{1,0:T(8,128)(2,1)} %param.10) | copy-start | bytes 6291460
  153.4 1.7 copy-start.1
  153.4 3.7 %copy-start.2 = (bf16[1,64,8192]{2,1,0:T(8,128)(2,1)S(1)}, bf16[1,64,8192]{2,1,0:T(8,128)(2,1)}, u32[]{:S(2)}) copy-start(bf16[1,64,8192]{2,1,0:T(8,128)(2,1)} %all-gather.5.cloned.1.call-done) | copy-start | bytes 3145732
  163.6 151.9 %copy-start.3 = (bf16[1,64,2048]{2,1,0:T(8,128)(2,1)S(1)}, bf16[1,64,2048]{2,1,0:T(8,128)(2,1)}, u32[]{:S(2)}) copy-start(bf16[1,64,2048]{2,1,0:T(8,128)(2,1)} %param.15) | copy-start | bytes 786436
  163.7 151.9 %copy-start.4 = (bf16[1,64,2048]{2,1,0:T(8,128)(2,1)S(1)}, bf16[1,64,2048]{2,1,0:T(8,128)(2,1)}, u32[]{:S(2)}) copy-start(bf16[1,64,2048]{2,1,0:T(8,128)(2,1)} %param.14) | copy-start | bytes 786436
  163.7 151.9 %copy-start.5 = (bf16[1,64,2048]{2,1,0:T(8,128)(2,1)S(1)}, bf16[1,64,2048]{2,1,0:T(8,128)(2,1)}, u32[]{:S(2)}) copy-start(bf16[1,64,2048]{2,1,0:T(8,128)(2,1)} %param.17) | copy-start | bytes 786436
  163.7 151.9 %copy-start.6 = (bf16[1,64,2048]{2,1,0:T(8,128)(2,1)S(1)}, bf16[1,64,2048]{2,1,0:T(8,128)(2,1)}, u32[]{:S(2)}) copy-start(bf16[1,64,2048]{2,1,0:T(8,128)(2,1)} %param.16) | copy-start | bytes 786436
Sparse Core Ops, SparseCore 0:
  9.6 28.8 all-gather.2
  40.0 27.4 all-gather.4
  163.8 151.7 all-reduce.2
where the time goes:
time: 329 us; the launch traced here: 325 us
  waiting for transfers between devices  198 us (60%)
  blocking collectives  81.3 us (25%)
  matrix products  19.1 us (6%)
  between operations  13.8 us (4%)
  other arithmetic  5.74 us (2%)
  starting transfers between devices  5.07 us (2%)
    psum x1, waiting for transfers between devices, body(): summed_down, summed_up = lax.psum((down_grad, up_gradient), 'dp')  151 us
    all_to_all x1, blocking collectives, body(): lax.all_to_all(adapter_output.reshape(owner_index, slot_capacity, model_w...  41 us
    all_to_all x1, blocking collectives, body(): lax.all_to_all(spread(shifted_index.astype(jnp.bfloat16)), 'owner', split...  40.3 us
    all_gather x1, waiting for transfers between devices, body(): lax.all_gather(adapter_down_weight, 'dp', axis=2, tiled=True)  19.7 us
    all_to_all x1, waiting for transfers between devices, body(): lax.all_to_all(spread(tokens), 'owner', split_axis=0, concat_axis=0, tile...  13.9 us
    all_gather x1, waiting for transfers between devices, body(): lax.all_gather(adapter_up_weight, 'dp', axis=2, tiled=True)  11.8 us
  transfers between devices with their start and end apart: 4, of which 4 were waited for; matrix products, arithmetic and copies ran while one was open for 3% of the time, Pallas kernels for 0%

commit v1 on v0

--- a/solution.py
+++ b/solution.py
@@ -1,6 +1,10 @@
+import functools
+
 import jax
 import jax.numpy as jnp
 from jax import lax
+from jax.experimental import pallas as pl
+from jax.experimental.pallas import tpu as pltpu
 from jax.sharding import PartitionSpec as P
 
 adapter_scale = 0.5
@@ -13,7 +17,7 @@
     return first_new / (jnp.sqrt(second_new) + adam_eps)
 
 
-def body(
+def plain_body(
     tokens,
     residual,
     token_adapter_index,
@@ -33,7 +37,10 @@
     member = (route_ids[:, None] == jnp.arange(owner_index, dtype=jnp.int32)[None, :]).astype(
         jnp.int32
     )
-    before = jnp.cumsum(member, axis=0) - member
+    earlier = jnp.tril(jnp.ones((tok_rows, tok_rows), jnp.bfloat16), -1)
+    before = jnp.dot(
+        earlier, member.astype(jnp.bfloat16), preferred_element_type=jnp.float32
+    ).astype(jnp.int32)
     within = jnp.sum(before * member, axis=1)
     target = route_ids * slot_capacity + within
     dispatch = (
@@ -104,7 +111,401 @@
     return (down_update[None], up_update[None], token_loss)
 
 
+MESH = pl.DeviceIdType.MESH
+F32, BF16 = jnp.float32, jnp.bfloat16
+FOLD = 2
+
+
+def dot_rows(a, b):
+    return lax.dot_general(a, b, (((1,), (1,)), ((), ())), preferred_element_type=F32)
+
+
+def dot_sum(a, b):
+    return lax.dot_general(a, b, (((0,), (0,)), ((), ())), preferred_element_type=F32)
+
+
+def kernel(
+    sizes,
+    ids_ref,
+    tok_ref,
+    res_ref,
+    down_ref,
+    up_ref,
+    down_first,
+    down_second,
+    up_first,
+    up_second,
+    down_out,
+    up_out,
+    loss_out,
+    tok_placed,
+    res_placed,
+    tok_here,
+    res_here,
+    down_all,
+    up_all,
+    up_sum,
+    down_sum,
+    up_part,
+    down_part,
+    up_heard,
+    down_heard,
+    loss_part,
+    loss_heard,
+    tok_send,
+    tok_recv,
+    res_send,
+    res_recv,
+    weight_send,
+    weight_recv,
+    grad_send,
+    grad_recv,
+    loss_send,
+    loss_recv,
+    own_sem,
+):
+    n_dp, n_owner, cap, rank, parts = sizes
+    slab = FOLD * cap
+    rows = n_owner * slab
+    toks, width = tok_ref.shape
+    half = width // FOLD
+    span = width // n_dp
+    step = half // parts
+    per = half // span
+    d, o = lax.axis_index("dp"), lax.axis_index("owner")
+
+    def flipped(k):
+        peer, bit = 0, 1
+        while bit < n_owner:
+            own = (o // bit) % 2
+            peer = peer + bit * ((own + (k // bit) % 2) % 2)
+            bit *= 2
+        return peer
+
+    peers = [flipped(k) for k in range(1, n_owner)]
+    others = [lax.rem(d + k, n_dp) for k in range(1, n_dp)]
+
+    barrier = pltpu.get_barrier_semaphore()
+    for p in peers:
+        pl.semaphore_signal(barrier, inc=1, device_id=(d, p), device_id_type=MESH)
+    for q in others:
+        pl.semaphore_signal(barrier, inc=1, device_id=(q, o), device_id_type=MESH)
+
+    ids = ids_ref[...]
+    member = (lax.broadcasted_iota(jnp.int32, (n_owner, toks), 0) == ids).astype(F32)
+    upper = (
+        lax.broadcasted_iota(jnp.int32, (toks, toks), 0)
+        < lax.broadcasted_iota(jnp.int32, (toks, toks), 1)
+    ).astype(F32)
+    before = jnp.dot(member.astype(BF16), upper.astype(BF16), preferred_element_type=F32)
+    within = jnp.sum(before * member, axis=0, keepdims=True)
+    target = ids.astype(F32) * float(slab) + within
+    row = lax.broadcasted_iota(jnp.int32, (rows, toks), 0).astype(F32)
+    first_half = (row == target).astype(F32)
+    second_half = (row == target + float(cap)).astype(F32)
+    home = first_half + second_half
+    dispatch = jnp.concatenate([first_half.astype(BF16), second_half.astype(BF16)], axis=1)
+
+    def place(src, dst, c):
+        two = jnp.concatenate(
+            [src[:, c * step : (c + 1) * step], src[:, half + c * step : half + (c + 1) * step]],
+            axis=0,
+        )
+        dst[c] = jnp.dot(dispatch, two, preferred_element_type=F32).astype(BF16)
+
+    mine = pl.ds(pl.multiple_of(o * slab, 16), slab)
+
+    def to_owner(placed, here, send, recv, k, p, c):
+        return pltpu.make_async_remote_copy(
+            src_ref=placed.at[c, pl.ds(pl.multiple_of(p * slab, 16), slab)],
+            dst_ref=here.at[c, mine],
+            send_sem=send.at[k, c],
+            recv_sem=recv.at[k, c],
+            device_id=(d, p),
+            device_id_type=MESH,
+        )
+
+    def slice_of(ref, q):
+        return ref.at[
+            pl.ds(pl.multiple_of((q // per) * rank, 16), rank),
+            pl.ds(pl.multiple_of((q % per) * span, 128), span),
+        ]
+
+    def weight_to(w, src, dst, k, q):
+        return pltpu.make_async_remote_copy(
+            src_ref=src,
+            dst_ref=slice_of(dst, d),
+            send_sem=weight_send.at[w, k],
+            recv_sem=weight_recv.at[w, d],
+            device_id=(q, o),
+            device_id_type=MESH,
+        )
+
+    own = [
+        pltpu.make_async_copy(down_ref, slice_of(down_all, d), own_sem.at[0]),
+        pltpu.make_async_copy(up_ref, slice_of(up_all, d), own_sem.at[1]),
+    ]
+    for copy in own:
+        copy.start()
+    own_tok = [
+        pltpu.make_async_copy(tok_placed.at[c, mine], tok_here.at[c, mine], own_sem.at[2 + c])
+        for c in range(parts)
+    ]
+    own_res = [
+        pltpu.make_async_copy(
+            res_placed.at[c, mine], res_here.at[c, mine], own_sem.at[2 + parts + c]
+        )
+        for c in range(parts)
+    ]
+
+    place(tok_ref, tok_placed, 0)
+    pl.semaphore_wait(barrier, len(peers) + len(others))
+
+    weights = [
+        [weight_to(w, src, dst, k, q) for k, q in enumerate(others)]
+        for w, (src, dst) in enumerate(((down_ref, down_all), (up_ref, up_all)))
+    ]
+    tok_copies = [
+        [to_owner(tok_placed, tok_here, tok_send, tok_recv, k, p, c) for k, p in enumerate(peers)]
+        for c in range(parts)
+    ]
+    res_copies = [
+        [to_owner(res_placed, res_here, res_send, res_recv, k, p, c) for k, p in enumerate(peers)]
+        for c in range(parts)
+    ]
+    for c in range(parts):
+        if c:
+            place(tok_ref, tok_placed, c)
+        for copy in tok_copies[c]:
+            copy.start()
+        own_tok[c].start()
+        if c == 0:
+            for copy in weights[0]:
+                copy.start()
+    for copy in weights[1]:
+        copy.start()
+    for c in range(parts):
+        place(res_ref, res_placed, c)
+        for copy in res_copies[c]:
+            copy.start()
+        own_res[c].start()
+
+    def weight_arrived(w, dst):
+        for q in others:
+            pltpu.make_async_remote_copy(
+                src_ref=slice_of(dst, q),
+                dst_ref=slice_of(dst, q),
+                send_sem=weight_send.at[w, 0],
+                recv_sem=weight_recv.at[w, q],
+                device_id=(q, o),
+                device_id_type=MESH,
+            ).wait_recv()
+        own[w].wait()
+
+    cols = lambda c: slice(c * step, (c + 1) * step)
+    fold_row = (lax.broadcasted_iota(jnp.int32, (rows, FOLD * rank), 0) % slab) // cap
+    fold_lane = lax.broadcasted_iota(jnp.int32, (rows, FOLD * rank), 1) // rank
+    same = (fold_row == fold_lane).astype(F32)
+
+    def folded(total, scale):
+        kept = total * same
+        both = kept + pltpu.roll(kept, rank, 1)
+        both = both.reshape(n_owner, FOLD, cap, FOLD * rank)
+        whole = both[:, 0] + both[:, 1]
+        whole = jnp.stack([whole, whole], axis=1).reshape(rows, FOLD * rank)
+        return (scale * whole * same).astype(BF16)
+
+    weight_arrived(0, down_all)
+    total = jnp.zeros((rows, FOLD * rank), F32)
+    for c in range(parts):
+        for copy in tok_copies[c]:
+            copy.wait_recv()
+        own_tok[c].wait()
+        total = total + dot_rows(tok_here[c], down_all[:, cols(c)])
+    hidden = folded(total, 1.0)
+
+    weight_arrived(1, up_all)
+
+    def grad_to(w, part, heard, q):
+        return pltpu.make_async_remote_copy(
+            src_ref=slice_of(part, q),
+            dst_ref=heard.at[d],
+            send_sem=grad_send.at[w, q],
+            recv_sem=grad_recv.at[w, d],
+            device_id=(q, o),
+            device_id_type=MESH,
+        )
+
+    def send_group(w, part, heard, g):
+        for q in range(g, n_dp, per):
+
+            @pl.when(d != q)
+            def _():
+                grad_to(w, part, heard, q).start()
+
+    ahead = parts // per
+    loss_part[...] = jnp.zeros((rows, 128), F32)
+    total = jnp.zeros((rows, FOLD * rank), F32)
+    for c in range(parts):
+        for copy in res_copies[c]:
+            copy.wait_recv()
+        own_res[c].wait()
+        up_c = up_all[:, cols(c)]
+        added = (adapter_scale * jnp.dot(hidden, up_c, preferred_element_type=F32)).astype(BF16)
+        shifted = res_here[c].astype(F32) + added.astype(F32)
+        square = shifted * shifted
+        lanes = square[:, :128]
+        for j in range(1, step // 128):
+            lanes = lanes + square[:, j * 128 : (j + 1) * 128]
+        loss_part[...] += lanes
+        cotangent = shifted.astype(BF16)
+        total = total + dot_rows(cotangent, up_c)
+        up_c_grad = adapter_scale * dot_sum(hidden, cotangent)
+        up_sum[:, cols(c)] = up_c_grad
+        up_part[:, cols(c)] = up_c_grad.astype(BF16)
+        if (c + 1) % ahead == 0:
+            send_group(0, up_part, up_heard, c // ahead)
+    hidden_grad = folded(total, adapter_scale)
+
+    for c in range(parts):
+        down_c_grad = dot_sum(hidden_grad, tok_here[c])
+        down_sum[:, cols(c)] = down_c_grad
+        down_part[:, cols(c)] = down_c_grad.astype(BF16)
+        if (c + 1) % ahead == 0:
+            send_group(1, down_part, down_heard, c // ahead)
+
+    def loss_to(k, p):
+        return pltpu.make_async_remote_copy(
+            src_ref=loss_part.at[pl.ds(pl.multiple_of(p * slab, 8), slab)],
+            dst_ref=loss_heard.at[mine],
+            send_sem=loss_send.at[k],
+            recv_sem=loss_recv.at[k],
+            device_id=(d, p),
+            device_id_type=MESH,
+        )
+
+    loss_copies = [loss_to(k, p) for k, p in enumerate(peers)]
+    for copy in loss_copies:
+        copy.start()
+    loss_heard[mine, :] = loss_part[mine, :]
+
+    def finish(w, part, heard, summed, first, second, out):
+        for q in others:
+            pltpu.make_async_remote_copy(
+                src_ref=heard.at[q],
+                dst_ref=heard.at[q],
+                send_sem=grad_send.at[w, q],
+                recv_sem=grad_recv.at[w, q],
+                device_id=(q, o),
+                device_id_type=MESH,
+            ).wait_recv()
+        grad = slice_of(summed, d)[...]
+        for q in others:
+            grad = grad + heard[q].astype(F32)
+        out[...] = adam_update(grad, first[...], second[...])
+
+    finish(0, up_part, up_heard, up_sum, up_first, up_second, up_out)
+
+    for copy in loss_copies:
+        copy.wait_recv()
+    sums = jnp.sum(loss_heard[...], axis=1, keepdims=True)
+    loss_out[...] = (0.5 / width) * jnp.sum(home * sums, axis=0, keepdims=True)
+
+    finish(1, down_part, down_heard, down_sum, down_first, down_second, down_out)
+
+    for group in weights + tok_copies + res_copies + [loss_copies]:
+        for copy in group:
+            copy.wait_send()
+    for w, part, heard in ((0, up_part, up_heard), (1, down_part, down_heard)):
+        for q in others:
+            grad_to(w, part, heard, q).wait_send()
+
+
+def kernel_body(
+    n_dp,
+    n_owner,
+    cap,
+    tokens,
+    residual,
+    token_adapter_index,
+    adapter_down_weight,
+    adapter_up_weight,
+    down_moment_first,
+    down_moment_second,
+    up_moment_first,
+    up_moment_second,
+):
+    toks, width = tokens.shape
+    _, rank, span = adapter_down_weight.shape
+    half, parts = width // FOLD, 4
+    step = half // parts
+    slab = FOLD * cap
+    rows = n_owner * slab
+    dma = pltpu.SemaphoreType.DMA
+    down_update, up_update, token_loss = pl.pallas_call(
+        functools.partial(kernel, (n_dp, n_owner, cap, rank, parts)),
+        out_shape=(
+            jax.ShapeDtypeStruct((rank, span), F32),
+            jax.ShapeDtypeStruct((rank, span), F32),
+            jax.ShapeDtypeStruct((1, toks), F32),
+        ),
+        in_specs=[pl.BlockSpec(memory_space=pltpu.VMEM)] * 9,
+        out_specs=[pl.BlockSpec(memory_space=pltpu.VMEM)] * 3,
+        scratch_shapes=[
+            pltpu.VMEM((parts, rows, step), BF16),
+            pltpu.VMEM((parts, rows, step), BF16),
+            pltpu.VMEM((parts, rows, step), BF16),
+            pltpu.VMEM((parts, rows, step), BF16),
+            pltpu.VMEM((FOLD * rank, half), BF16),
+            pltpu.VMEM((FOLD * rank, half), BF16),
+            pltpu.VMEM((FOLD * rank, half), F32),
+            pltpu.VMEM((FOLD * rank, half), F32),
+            pltpu.VMEM((FOLD * rank, half), BF16),
+            pltpu.VMEM((FOLD * rank, half), BF16),
+            pltpu.VMEM((n_dp, rank, span), BF16),
+            pltpu.VMEM((n_dp, rank, span), BF16),
+            pltpu.VMEM((rows, 128), F32),
+            pltpu.VMEM((rows, 128), F32),
+            dma((n_owner - 1, parts)),
+            dma((n_owner - 1, parts)),
+            dma((n_owner - 1, parts)),
+            dma((n_owner - 1, parts)),
+            dma((2, n_dp)),
+            dma((2, n_dp)),
+            dma((2, n_dp)),
+            dma((2, n_dp)),
+            dma((n_owner - 1,)),
+            dma((n_owner - 1,)),
+            dma((2 + 2 * parts,)),
+        ],
+        compiler_params=pltpu.CompilerParams(
+            collective_id=0, has_side_effects=True, vmem_limit_bytes=52 * 2**20
+        ),
+        name="step",
+    )(
+        token_adapter_index.reshape(1, toks),
+        tokens,
+        residual,
+        adapter_down_weight[0],
+        adapter_up_weight[0],
+        down_moment_first[0],
+        down_moment_second[0],
+        up_moment_first[0],
+        up_moment_second[0],
+    )
+    return (down_update[None], up_update[None], token_loss[0])
+
+
 def solution(mesh):
+    n_dp, n_owner = mesh.shape["dp"], mesh.shape["owner"]
+
+    def body(*arrays):
+        toks = arrays[0].shape[0]
+        cap = max(2, 3 * toks // (2 * n_owner))
+        if cap % 8 == 0 and FOLD * cap % 16 == 0 and n_dp % FOLD == 0 and FOLD * 2 == n_dp:
+            return kernel_body(n_dp, n_owner, cap, *arrays)
+        return plain_body(*arrays)
+
     return jax.shard_map(
         body,
         mesh=mesh,

time: 329 us -> 126 us (0.38); the launches traced: 325 us -> 125 us
  waiting for transfers between devices: 198 us -> 0 us
  Pallas kernels: 0 us -> 114 us
  blocking collectives: 81.3 us -> 0 us
  matrix products: 19.1 us -> 0 us
  between operations: 13.8 us -> 0.66 us
  local copies, waits for them, and re-layouts: 1.71 us -> 10.6 us
  other arithmetic: 5.74 us -> 0 us
  starting transfers between devices: 5.07 us -> 0 us
    psum x1 -> x0, waiting for transfers between devices: 151 us -> none  [body(): summed_down, summed_up = lax.psum((down_grad, up_gradient), 'dp')]
    pallas_call x0 -> x1, Pallas kernels: none -> 114 us  [kernel_body(): pl.pallas_call(functools.partial(kernel, (n_dp, n_owner, cap, rank, parts...]
    all_to_all x2 -> x0, blocking collectives: 81.3 us -> none  [the longest x1 41 us: body(): lax.all_to_all(adapter_output.reshape(owner_index, slot_capacity, model_w...]
    all_gather x2 -> x0, waiting for transfers between devices: 31.5 us -> none  [the longest x1 19.7 us: body(): lax.all_gather(adapter_down_weight, 'dp', axis=2, tiled=True)]
    dot_general x7 -> x0, matrix products: 19.1 us -> none  [the longest x1 6.54 us: body(): lax.dot_general(hidden_gradient, arrived, (((0,), (0,)), ((), ())), prefe...]
    all_to_all x1 -> x0, waiting for transfers between devices: 13.9 us -> none  [body(): lax.all_to_all(spread(tokens), 'owner', split_axis=0, concat_axis=0, tile...]
    unnamed x16 -> x17, local copies, waits for them, and re-layouts: 1.71 us -> 10.6 us
    all_to_all x1 -> x0, starting transfers between devices: 4.99 us -> none  [body(): lax.all_to_all(spread(tokens), 'owner', split_axis=0, concat_axis=0, tile...]
  transfers between devices with their start and end apart: 4 -> 0, of which waited for: 4 -> 0; matrix products, arithmetic and copies ran while one was open for 3% -> 0% of each run, Pallas kernels for 0% -> 0%
where the time goes in v1:
time: 126 us; the launch traced here: 125 us
  Pallas kernels  114 us (90%)
  local copies, waits for them, and re-layouts  10.6 us (8%)
    pallas_call x1, Pallas kernels, kernel_body(): pl.pallas_call(functools.partial(kernel, (n_dp, n_owner, cap, rank, parts...  114 us
    unnamed x17, local copies, waits for them, and re-layouts  10.6 us

profile of v1, /device:TPU:9, one launch (start us, length us, event | category | flops | bytes accessed | tf_op | source)
XLA Modules:
  0.0 125.3 jit_solution(189311883594692829)
XLA Ops:
  0.6 0.0 copy-start
  0.6 0.9 copy-done
  1.6 0.0 copy-start.1
  1.6 0.9 copy-done.1
  2.5 0.0 copy-start.2
  2.5 0.9 copy-done.2
  3.5 0.0 copy-start.3
  3.5 0.9 copy-done.3
  4.4 0.0 copy-start.4
  4.4 0.9 copy-done.4
  5.4 0.0 copy-start.5
  5.4 0.9 copy-done.5
  6.3 0.0 copy-start.6
  6.3 0.7 copy-done.6
  7.0 114.0 %step.1 = (f32[64,2048]{1,0:T(8,128)}, f32[64,2048]{1,0:T(8,128)}, f32[1,128]{1,0:T(1,128)S(1)}) custom-call(s32[1,128]{1,0:T(1,128)S(1)} %bitcast.16, bf16[128,8192]{1,0:T(8,128)(2,1)} %tok_ref.1, bf16[128,8192]{1,0:T(8,128)(2,1)} %res_ref.1, bf16[64,2048]{1,0:T(8,128)(2,1)S(1)} %bitcast.10, bf16[64,2048]{1,0:T(8,128)(2,1)S(1)} %bitcast.11, ...), custom_call_target="tpu_custom_call" | custom-call | tf_op jit(solution)/shard_map/step/pallas_call | solution.py:445
  121.0 1.9 %copy.15 = f32[1,64,2048]{2,1,0:T(8,128)} copy(f32[1,64,2048]{2,1,0:T(8,128)} %bitcast.19) | data formatting | bytes 1048576
  122.9 1.9 %copy.16 = f32[1,64,2048]{2,1,0:T(8,128)} copy(f32[1,64,2048]{2,1,0:T(8,128)} %bitcast.18) | data formatting | bytes 1048576
  124.8 0.5 copy.17
Async XLA Ops:
  0.6 1.0 copy-start
  1.6 0.9 copy-start.1
  2.5 0.9 copy-start.2
  3.5 0.9 copy-start.3
  4.4 0.9 copy-start.4
  5.4 0.9 copy-start.5
  6.3 0.7 copy-start.6

commit v2 on v1

--- a/solution.py
+++ b/solution.py
@@ -131,13 +131,11 @@
     res_ref,
     down_ref,
     up_ref,
-    down_first,
-    down_second,
-    up_first,
-    up_second,
     down_out,
     up_out,
     loss_out,
+    tok_in,
+    res_in,
     tok_placed,
     res_placed,
     tok_here,
@@ -163,6 +161,7 @@
     loss_send,
     loss_recv,
     own_sem,
+    in_sem,
 ):
     n_dp, n_owner, cap, rank, parts = sizes
     slab = FOLD * cap
@@ -182,14 +181,35 @@
             bit *= 2
         return peer
 
-    peers = [flipped(k) for k in range(1, n_owner)]
+    near = sorted(range(1, n_owner), key=lambda k: (k % 2, -k))
+    peers = [flipped(k) for k in near]
     others = [lax.rem(d + k, n_dp) for k in range(1, n_dp)]
+
+    def slice_of(ref, q):
+        return ref.at[
+            pl.ds(pl.multiple_of((q // per) * rank, 16), rank),
+            pl.ds(pl.multiple_of((q % per) * span, 128), span),
+        ]
 
     barrier = pltpu.get_barrier_semaphore()
     for p in peers:
         pl.semaphore_signal(barrier, inc=1, device_id=(d, p), device_id_type=MESH)
     for q in others:
         pl.semaphore_signal(barrier, inc=1, device_id=(q, o), device_id_type=MESH)
+
+    loads = [
+        pltpu.make_async_copy(src, dst, in_sem.at[i])
+        for i, (src, dst) in enumerate(
+            (
+                (down_ref, slice_of(down_all, d)),
+                (tok_ref, tok_in),
+                (up_ref, slice_of(up_all, d)),
+                (res_ref, res_in),
+            )
+        )
+    ]
+    for load in loads:
+        load.start()
 
     ids = ids_ref[...]
     member = (lax.broadcasted_iota(jnp.int32, (n_owner, toks), 0) == ids).astype(F32)
@@ -225,15 +245,9 @@
             device_id_type=MESH,
         )
 
-    def slice_of(ref, q):
-        return ref.at[
-            pl.ds(pl.multiple_of((q // per) * rank, 16), rank),
-            pl.ds(pl.multiple_of((q % per) * span, 128), span),
-        ]
-
-    def weight_to(w, src, dst, k, q):
+    def weight_to(w, dst, k, q):
         return pltpu.make_async_remote_copy(
-            src_ref=src,
+            src_ref=slice_of(dst, d),
             dst_ref=slice_of(dst, d),
             send_sem=weight_send.at[w, k],
             recv_sem=weight_recv.at[w, d],
@@ -241,29 +255,20 @@
             device_id_type=MESH,
         )
 
-    own = [
-        pltpu.make_async_copy(down_ref, slice_of(down_all, d), own_sem.at[0]),
-        pltpu.make_async_copy(up_ref, slice_of(up_all, d), own_sem.at[1]),
-    ]
-    for copy in own:
-        copy.start()
     own_tok = [
-        pltpu.make_async_copy(tok_placed.at[c, mine], tok_here.at[c, mine], own_sem.at[2 + c])
+        pltpu.make_async_copy(tok_placed.at[c, mine], tok_here.at[c, mine], own_sem.at[c])
         for c in range(parts)
     ]
     own_res = [
         pltpu.make_async_copy(
-            res_placed.at[c, mine], res_here.at[c, mine], own_sem.at[2 + parts + c]
+            res_placed.at[c, mine], res_here.at[c, mine], own_sem.at[parts + c]
         )
         for c in range(parts)
     ]
 
-    place(tok_ref, tok_placed, 0)
-    pl.semaphore_wait(barrier, len(peers) + len(others))
-
     weights = [
-        [weight_to(w, src, dst, k, q) for k, q in enumerate(others)]
-        for w, (src, dst) in enumerate(((down_ref, down_all), (up_ref, up_all)))
+        [weight_to(w, dst, k, q) for k, q in enumerate(others)]
+        for w, dst in enumerate((down_all, up_all))
     ]
     tok_copies = [
         [to_owner(tok_placed, tok_here, tok_send, tok_recv, k, p, c) for k, p in enumerate(peers)]
@@ -273,19 +278,24 @@
         [to_owner(res_placed, res_here, res_send, res_recv, k, p, c) for k, p in enumerate(peers)]
         for c in range(parts)
     ]
+    loads[1].wait()
+    place(tok_in, tok_placed, 0)
+    loads[0].wait()
+    pl.semaphore_wait(barrier, len(peers) + len(others))
+    for copy in weights[0]:
+        copy.start()
     for c in range(parts):
         if c:
-            place(tok_ref, tok_placed, c)
+            place(tok_in, tok_placed, c)
         for copy in tok_copies[c]:
             copy.start()
         own_tok[c].start()
-        if c == 0:
-            for copy in weights[0]:
-                copy.start()
+    loads[2].wait()
     for copy in weights[1]:
         copy.start()
+    loads[3].wait()
     for c in range(parts):
-        place(res_ref, res_placed, c)
+        place(res_in, res_placed, c)
         for copy in res_copies[c]:
             copy.start()
         own_res[c].start()
@@ -300,7 +310,6 @@
                 device_id=(q, o),
                 device_id_type=MESH,
             ).wait_recv()
-        own[w].wait()
 
     cols = lambda c: slice(c * step, (c + 1) * step)
     fold_row = (lax.broadcasted_iota(jnp.int32, (rows, FOLD * rank), 0) % slab) // cap
@@ -326,24 +335,28 @@
 
     weight_arrived(1, up_all)
 
-    def grad_to(w, part, heard, q):
+    ahead = parts // per
+
+    def grad_to(w, part, heard, q, j):
         return pltpu.make_async_remote_copy(
-            src_ref=slice_of(part, q),
-            dst_ref=heard.at[d],
-            send_sem=grad_send.at[w, q],
-            recv_sem=grad_recv.at[w, d],
+            src_ref=part.at[
+                pl.ds(pl.multiple_of((q // per) * rank, 16), rank),
+                pl.ds(pl.multiple_of((q % per) * span + j * step, 128), step),
+            ],
+            dst_ref=heard.at[d, j],
+            send_sem=grad_send.at[w, q, j],
+            recv_sem=grad_recv.at[w, d, j],
             device_id=(q, o),
             device_id_type=MESH,
         )
 
-    def send_group(w, part, heard, g):
-        for q in range(g, n_dp, per):
+    def send_piece(w, part, heard, c):
+        for q in range(c // ahead, n_dp, per):
 
             @pl.when(d != q)
             def _():
-                grad_to(w, part, heard, q).start()
-
-    ahead = parts // per
+                grad_to(w, part, heard, q, c % ahead).start()
+
     loss_part[...] = jnp.zeros((rows, 128), F32)
     total = jnp.zeros((rows, FOLD * rank), F32)
     for c in range(parts):
@@ -363,16 +376,14 @@
         up_c_grad = adapter_scale * dot_sum(hidden, cotangent)
         up_sum[:, cols(c)] = up_c_grad
         up_part[:, cols(c)] = up_c_grad.astype(BF16)
-        if (c + 1) % ahead == 0:
-            send_group(0, up_part, up_heard, c // ahead)
+        send_piece(0, up_part, up_heard, c)
     hidden_grad = folded(total, adapter_scale)
 
     for c in range(parts):
         down_c_grad = dot_sum(hidden_grad, tok_here[c])
         down_sum[:, cols(c)] = down_c_grad
         down_part[:, cols(c)] = down_c_grad.astype(BF16)
-        if (c + 1) % ahead == 0:
-            send_group(1, down_part, down_heard, c // ahead)
+        send_piece(1, down_part, down_heard, c)
 
     def loss_to(k, p):
         return pltpu.make_async_remote_copy(
@@ -389,36 +400,41 @@
         copy.start()
     loss_heard[mine, :] = loss_part[mine, :]
 
-    def finish(w, part, heard, summed, first, second, out):
-        for q in others:
-            pltpu.make_async_remote_copy(
-                src_ref=heard.at[q],
-                dst_ref=heard.at[q],
-                send_sem=grad_send.at[w, q],
-                recv_sem=grad_recv.at[w, q],
-                device_id=(q, o),
-                device_id_type=MESH,
-            ).wait_recv()
-        grad = slice_of(summed, d)[...]
-        for q in others:
-            grad = grad + heard[q].astype(F32)
-        out[...] = adam_update(grad, first[...], second[...])
-
-    finish(0, up_part, up_heard, up_sum, up_first, up_second, up_out)
+    def finish(w, heard, summed, out):
+        for j in range(ahead):
+            for q in others:
+                pltpu.make_async_remote_copy(
+                    src_ref=heard.at[q, j],
+                    dst_ref=heard.at[q, j],
+                    send_sem=grad_send.at[w, q, j],
+                    recv_sem=grad_recv.at[w, q, j],
+                    device_id=(q, o),
+                    device_id_type=MESH,
+                ).wait_recv()
+            grad = summed[
+                pl.ds(pl.multiple_of((d // per) * rank, 16), rank),
+                pl.ds(pl.multiple_of((d % per) * span + j * step, 128), step),
+            ]
+            for q in others:
+                grad = grad + heard[q, j].astype(F32)
+            out[:, j * step : (j + 1) * step] = grad
+
+    finish(0, up_heard, up_sum, up_out)
 
     for copy in loss_copies:
         copy.wait_recv()
     sums = jnp.sum(loss_heard[...], axis=1, keepdims=True)
-    loss_out[...] = (0.5 / width) * jnp.sum(home * sums, axis=0, keepdims=True)
-
-    finish(1, down_part, down_heard, down_sum, down_first, down_second, down_out)
+    loss_out[...] = jnp.sum(home * sums, axis=0, keepdims=True)
+
+    finish(1, down_heard, down_sum, down_out)
 
     for group in weights + tok_copies + res_copies + [loss_copies]:
         for copy in group:
             copy.wait_send()
     for w, part, heard in ((0, up_part, up_heard), (1, down_part, down_heard)):
         for q in others:
-            grad_to(w, part, heard, q).wait_send()
+            for j in range(ahead):
+                grad_to(w, part, heard, q, j).wait_send()
 
 
 def kernel_body(
@@ -439,19 +455,23 @@
     _, rank, span = adapter_down_weight.shape
     half, parts = width // FOLD, 4
     step = half // parts
+    pieces = span // step
     slab = FOLD * cap
     rows = n_owner * slab
     dma = pltpu.SemaphoreType.DMA
-    down_update, up_update, token_loss = pl.pallas_call(
+    down_grad, up_grad, row_loss = pl.pallas_call(
         functools.partial(kernel, (n_dp, n_owner, cap, rank, parts)),
         out_shape=(
             jax.ShapeDtypeStruct((rank, span), F32),
             jax.ShapeDtypeStruct((rank, span), F32),
             jax.ShapeDtypeStruct((1, toks), F32),
         ),
-        in_specs=[pl.BlockSpec(memory_space=pltpu.VMEM)] * 9,
+        in_specs=[pl.BlockSpec(memory_space=pltpu.VMEM)]
+        + [pl.BlockSpec(memory_space=pltpu.HBM)] * 4,
         out_specs=[pl.BlockSpec(memory_space=pltpu.VMEM)] * 3,
         scratch_shapes=[
+            pltpu.VMEM((toks, width), BF16),
+            pltpu.VMEM((toks, width), BF16),
             pltpu.VMEM((parts, rows, step), BF16),
             pltpu.VMEM((parts, rows, step), BF16),
             pltpu.VMEM((parts, rows, step), BF16),
@@ -462,8 +482,8 @@
             pltpu.VMEM((FOLD * rank, half), F32),
             pltpu.VMEM((FOLD * rank, half), BF16),
             pltpu.VMEM((FOLD * rank, half), BF16),
-            pltpu.VMEM((n_dp, rank, span), BF16),
-            pltpu.VMEM((n_dp, rank, span), BF16),
+            pltpu.VMEM((n_dp, pieces, rank, step), BF16),
+            pltpu.VMEM((n_dp, pieces, rank, step), BF16),
             pltpu.VMEM((rows, 128), F32),
             pltpu.VMEM((rows, 128), F32),
             dma((n_owner - 1, parts)),
@@ -472,11 +492,12 @@
             dma((n_owner - 1, parts)),
             dma((2, n_dp)),
             dma((2, n_dp)),
-            dma((2, n_dp)),
-            dma((2, n_dp)),
+            dma((2, n_dp, pieces)),
+            dma((2, n_dp, pieces)),
             dma((n_owner - 1,)),
             dma((n_owner - 1,)),
-            dma((2 + 2 * parts,)),
+            dma((2 * parts,)),
+            dma((4,)),
         ],
         compiler_params=pltpu.CompilerParams(
             collective_id=0, has_side_effects=True, vmem_limit_bytes=52 * 2**20
@@ -488,12 +509,10 @@
         residual,
         adapter_down_weight[0],
         adapter_up_weight[0],
-        down_moment_first[0],
-        down_moment_second[0],
-        up_moment_first[0],
-        up_moment_second[0],
-    )
-    return (down_update[None], up_update[None], token_loss[0])
+    )
+    down_update = adam_update(down_grad[None], down_moment_first, down_moment_second)
+    up_update = adam_update(up_grad[None], up_moment_first, up_moment_second)
+    return (down_update, up_update, (0.5 / width) * row_loss[0])
 
 
 def solution(mesh):

time: 126 us -> 111 us (0.88)
  Pallas kernels: 114 us -> 105 us
  local copies, waits for them, and re-layouts: 10.6 us -> 2.56 us
  other arithmetic: 0 us -> 2.14 us
    pallas_call x1, Pallas kernels: 114 us -> 105 us  [kernel_body(): pl.pallas_call(functools.partial(kernel, (n_dp, n_owner, cap, rank, parts...]
    unnamed x17 -> x14, local copies, waits for them, and re-layouts: 10.6 us -> 2.56 us
    div x0 -> x1, other arithmetic: none -> 1.63 us  [adam_update(): return first_new / (jnp.sqrt(second_new) + adam_eps)]
where the time goes in v2:
time: 111 us; the launch traced here: 110 us
  Pallas kernels  105 us (95%)
  local copies, waits for them, and re-layouts  2.56 us (2%)
  other arithmetic  2.14 us (2%)
    pallas_call x1, Pallas kernels, kernel_body(): pl.pallas_call(functools.partial(kernel, (n_dp, n_owner, cap, rank, parts...  105 us
    unnamed x14, local copies, waits for them, and re-layouts  2.56 us

profile of v2, /device:TPU:9, one launch (start us, length us, event | category | flops | bytes accessed | tf_op | source)
XLA Modules:
  0.0 110.4 jit_solution(11887735158284680823)
XLA Ops:
  0.6 0.0 copy-start
  0.6 0.9 copy-done
  1.6 0.0 copy-start.1
  1.6 0.9 copy-done.1
  2.5 0.0 copy-start.2
  2.5 0.7 copy-done.2
  3.2 0.0 copy-start.3
  3.2 0.0 copy-start.4
  3.2 0.0 copy-start.5
  3.2 0.0 copy-start.6
  3.2 105.0 %step.1 = (f32[64,2048]{1,0:T(8,128)S(1)}, f32[64,2048]{1,0:T(8,128)S(1)}, f32[1,128]{1,0:T(1,128)S(1)}) custom-call(s32[1,128]{1,0:T(1,128)S(1)} %bitcast.35, bf16[128,8192]{1,0:T(8,128)(2,1)} %tok_ref.1, bf16[128,8192]{1,0:T(8,128)(2,1)} %res_ref.1, bf16[64,2048]{1,0:T(8,128)(2,1)S(1)} %bitcast.33, bf16[64,2048]{1,0:T(8,128)(2,1)S(1)} %bitcast.34), custom_call_target="tpu_custom_call" | custom-call | tf_op jit(solution)/shard_map/step/pallas_call | solution.py:462
  108.2 0.0 copy-done.3
  108.2 0.0 copy-done.4
  108.2 0.0 copy-done.5
  108.2 0.0 copy-done.6
  108.2 1.6 %fusion.4 = (f32[1,64,2048]{2,1,0:T(8,128)}, f32[1,64,2048]{2,1,0:T(8,128)}) fusion(f32[64,2048]{1,0:T(8,128)S(1)} %get-tuple-element.6, bf16[1,64,2048]{2,1,0:T(8,128)(2,1)S(1)} %copy-done.3, bf16[1,64,2048]{2,1,0:T(8,128)(2,1)S(1)} %copy-done.4, f32[64,2048]{1,0:T(8,128)S(1)} %get-tuple-element.7, bf16[1,64,2048]{2,1,0:T(8,128)(2,1)S(1)} %copy-done.5, ...), kind=kLoop, calls=%fused_computation.6 | loop fusion | flops 2883584 | bytes 3145728 | tf_op jit(solution)/shard_map/div | solution.py:17
  109.9 0.5 multiply_bitcast_fusion
Async XLA Ops:
  0.6 1.0 copy-start
  1.6 0.9 copy-start.1
  2.5 0.7 copy-start.2
  3.2 105.0 %copy-start.3 = (bf16[1,64,2048]{2,1,0:T(8,128)(2,1)S(1)}, bf16[1,64,2048]{2,1,0:T(8,128)(2,1)}, u32[]{:S(2)}) copy-start(bf16[1,64,2048]{2,1,0:T(8,128)(2,1)} %param.15) | copy-start | bytes 786436
  3.2 105.0 %copy-start.4 = (bf16[1,64,2048]{2,1,0:T(8,128)(2,1)S(1)}, bf16[1,64,2048]{2,1,0:T(8,128)(2,1)}, u32[]{:S(2)}) copy-start(bf16[1,64,2048]{2,1,0:T(8,128)(2,1)} %param.14) | copy-start | bytes 786436
  3.2 105.0 %copy-start.5 = (bf16[1,64,2048]{2,1,0:T(8,128)(2,1)S(1)}, bf16[1,64,2048]{2,1,0:T(8,128)(2,1)}, u32[]{:S(2)}) copy-start(bf16[1,64,2048]{2,1,0:T(8,128)(2,1)} %param.17) | copy-start | bytes 786436
  3.2 105.0 %copy-start.6 = (bf16[1,64,2048]{2,1,0:T(8,128)(2,1)S(1)}, bf16[1,64,2048]{2,1,0:T(8,128)(2,1)}, u32[]{:S(2)}) copy-start(bf16[1,64,2048]{2,1,0:T(8,128)(2,1)} %param.16) | copy-start | bytes 786436

commit v3 on v2

--- a/solution.py
+++ b/solution.py
@@ -453,7 +453,7 @@
 ):
     toks, width = tokens.shape
     _, rank, span = adapter_down_weight.shape
-    half, parts = width // FOLD, 4
+    half, parts = width // FOLD, 8
     step = half // parts
     pieces = span // step
     slab = FOLD * cap

time: 111 us -> 109 us (0.982)
  Pallas kernels: 105 us -> 103 us
    pallas_call x1, Pallas kernels: 105 us -> 103 us  [kernel_body(): pl.pallas_call(functools.partial(kernel, (n_dp, n_owner, cap, rank, parts...]
where the time goes in v3:
time: 109 us; the launch traced here: 108 us
  Pallas kernels  103 us (94%)
  local copies, waits for them, and re-layouts  2.56 us (2%)
  other arithmetic  2.14 us (2%)
    pallas_call x1, Pallas kernels, kernel_body(): pl.pallas_call(functools.partial(kernel, (n_dp, n_owner, cap, rank, parts...  103 us
    unnamed x14, local copies, waits for them, and re-layouts  2.56 us

profile of v3, /device:TPU:9, one launch (start us, length us, event | category | flops | bytes accessed | tf_op | source)
XLA Modules:
  0.0 108.4 jit_solution(16124595588238662132)
XLA Ops:
  0.6 0.0 copy-start
  0.6 0.9 copy-done
  1.6 0.0 copy-start.1
  1.6 0.9 copy-done.1
  2.5 0.0 copy-start.2
  2.5 0.7 copy-done.2
  3.2 0.0 copy-start.3
  3.2 0.0 copy-start.4
  3.2 0.0 copy-start.5
  3.2 0.0 copy-start.6
  3.2 103.0 %step.1 = (f32[64,2048]{1,0:T(8,128)S(1)}, f32[64,2048]{1,0:T(8,128)S(1)}, f32[1,128]{1,0:T(1,128)S(1)}) custom-call(s32[1,128]{1,0:T(1,128)S(1)} %bitcast.35, bf16[128,8192]{1,0:T(8,128)(2,1)} %tok_ref.1, bf16[128,8192]{1,0:T(8,128)(2,1)} %res_ref.1, bf16[64,2048]{1,0:T(8,128)(2,1)S(1)} %bitcast.33, bf16[64,2048]{1,0:T(8,128)(2,1)S(1)} %bitcast.34), custom_call_target="tpu_custom_call" | custom-call | tf_op jit(solution)/shard_map/step/pallas_call | solution.py:462
  106.2 0.0 copy-done.3
  106.2 0.0 copy-done.4
  106.2 0.0 copy-done.5
  106.2 0.0 copy-done.6
  106.2 1.6 %fusion.4 = (f32[1,64,2048]{2,1,0:T(8,128)}, f32[1,64,2048]{2,1,0:T(8,128)}) fusion(f32[64,2048]{1,0:T(8,128)S(1)} %get-tuple-element.6, bf16[1,64,2048]{2,1,0:T(8,128)(2,1)S(1)} %copy-done.3, bf16[1,64,2048]{2,1,0:T(8,128)(2,1)S(1)} %copy-done.4, f32[64,2048]{1,0:T(8,128)S(1)} %get-tuple-element.7, bf16[1,64,2048]{2,1,0:T(8,128)(2,1)S(1)} %copy-done.5, ...), kind=kLoop, calls=%fused_computation.6 | loop fusion | flops 2883584 | bytes 3145728 | tf_op jit(solution)/shard_map/div | solution.py:17
  107.9 0.5 multiply_bitcast_fusion
Async XLA Ops:
  0.6 1.0 copy-start
  1.6 0.9 copy-start.1
  2.5 0.7 copy-start.2
  3.2 103.0 %copy-start.3 = (bf16[1,64,2048]{2,1,0:T(8,128)(2,1)S(1)}, bf16[1,64,2048]{2,1,0:T(8,128)(2,1)}, u32[]{:S(2)}) copy-start(bf16[1,64,2048]{2,1,0:T(8,128)(2,1)} %param.15) | copy-start | bytes 786436
  3.2 103.0 %copy-start.4 = (bf16[1,64,2048]{2,1,0:T(8,128)(2,1)S(1)}, bf16[1,64,2048]{2,1,0:T(8,128)(2,1)}, u32[]{:S(2)}) copy-start(bf16[1,64,2048]{2,1,0:T(8,128)(2,1)} %param.14) | copy-start | bytes 786436
  3.2 103.0 %copy-start.5 = (bf16[1,64,2048]{2,1,0:T(8,128)(2,1)S(1)}, bf16[1,64,2048]{2,1,0:T(8,128)(2,1)}, u32[]{:S(2)}) copy-start(bf16[1,64,2048]{2,1,0:T(8,128)(2,1)} %param.17) | copy-start | bytes 786436
  3.2 103.0 %copy-start.6 = (bf16[1,64,2048]{2,1,0:T(8,128)(2,1)S(1)}, bf16[1,64,2048]{2,1,0:T(8,128)(2,1)}, u32[]{:S(2)}) copy-start(bf16[1,64,2048]{2,1,0:T(8,128)(2,1)} %param.16) | copy-start | bytes 786436

commit v4 on v3

--- a/solution.py
+++ b/solution.py
@@ -145,9 +145,11 @@
     up_sum,
     down_sum,
     up_part,
-    down_part,
     up_heard,
-    down_heard,
+    near_part,
+    near_heard,
+    far_part,
+    far_heard,
     loss_part,
     loss_heard,
     tok_send,
@@ -162,6 +164,8 @@
     loss_recv,
     own_sem,
     in_sem,
+    relay_send,
+    relay_recv,
 ):
     n_dp, n_owner, cap, rank, parts = sizes
     slab = FOLD * cap
@@ -379,11 +383,26 @@
         send_piece(0, up_part, up_heard, c)
     hidden_grad = folded(total, adapter_scale)
 
-    for c in range(parts):
-        down_c_grad = dot_sum(hidden_grad, tok_here[c])
-        down_sum[:, cols(c)] = down_c_grad
-        down_part[:, cols(c)] = down_c_grad.astype(BF16)
-        send_piece(1, down_part, down_heard, c)
+    side = d % 2
+    partner, far = d + 1 - 2 * side, lax.rem(d + 2, n_dp)
+
+    def relay(i, src, dst, stage, q):
+        return pltpu.make_async_remote_copy(
+            src_ref=src.at[i],
+            dst_ref=dst.at[i],
+            send_sem=relay_send.at[stage, i],
+            recv_sem=relay_recv.at[stage, i],
+            device_id=(q, o),
+            device_id_type=MESH,
+        )
+
+    near_copies = [relay(i, near_part, near_heard, 0, partner) for i in range(ahead)]
+    far_copies = [relay(i, far_part, far_heard, 1, far) for i in range(ahead)]
+    for i in range(ahead):
+        near_part[i] = dot_sum(hidden_grad, tok_here[(1 - side) * ahead + i]).astype(BF16)
+        near_copies[i].start()
+    for i in range(ahead):
+        down_sum[i] = dot_sum(hidden_grad, tok_here[side * ahead + i])
 
     def loss_to(k, p):
         return pltpu.make_async_remote_copy(
@@ -419,6 +438,13 @@
                 grad = grad + heard[q, j].astype(F32)
             out[:, j * step : (j + 1) * step] = grad
 
+    for i in range(ahead):
+        near_copies[i].wait_recv()
+        down_sum[i] += near_heard[i].astype(F32)
+        far_row = pl.multiple_of((far // per) * rank, 16)
+        far_part[i] = down_sum[i, pl.ds(far_row, rank), :].astype(BF16)
+        far_copies[i].start()
+
     finish(0, up_heard, up_sum, up_out)
 
     for copy in loss_copies:
@@ -426,12 +452,16 @@
     sums = jnp.sum(loss_heard[...], axis=1, keepdims=True)
     loss_out[...] = jnp.sum(home * sums, axis=0, keepdims=True)
 
-    finish(1, down_heard, down_sum, down_out)
-
-    for group in weights + tok_copies + res_copies + [loss_copies]:
+    for i in range(ahead):
+        far_copies[i].wait_recv()
+        own_row = pl.multiple_of((d // per) * rank, 16)
+        own = down_sum[i, pl.ds(own_row, rank), :]
+        down_out[:, i * step : (i + 1) * step] = own + far_heard[i].astype(F32)
+
+    for group in weights + tok_copies + res_copies + [loss_copies, near_copies, far_copies]:
         for copy in group:
             copy.wait_send()
-    for w, part, heard in ((0, up_part, up_heard), (1, down_part, down_heard)):
+    for w, part, heard in ((0, up_part, up_heard),):
         for q in others:
             for j in range(ahead):
                 grad_to(w, part, heard, q, j).wait_send()
@@ -479,11 +509,13 @@
             pltpu.VMEM((FOLD * rank, half), BF16),
             pltpu.VMEM((FOLD * rank, half), BF16),
             pltpu.VMEM((FOLD * rank, half), F32),
-            pltpu.VMEM((FOLD * rank, half), F32),
-            pltpu.VMEM((FOLD * rank, half), BF16),
+            pltpu.VMEM((pieces, FOLD * rank, step), F32),
             pltpu.VMEM((FOLD * rank, half), BF16),
             pltpu.VMEM((n_dp, pieces, rank, step), BF16),
-            pltpu.VMEM((n_dp, pieces, rank, step), BF16),
+            pltpu.VMEM((pieces, FOLD * rank, step), BF16),
+            pltpu.VMEM((pieces, FOLD * rank, step), BF16),
+            pltpu.VMEM((pieces, rank, step), BF16),
+            pltpu.VMEM((pieces, rank, step), BF16),
             pltpu.VMEM((rows, 128), F32),
             pltpu.VMEM((rows, 128), F32),
             dma((n_owner - 1, parts)),
@@ -498,6 +530,8 @@
             dma((n_owner - 1,)),
             dma((2 * parts,)),
             dma((4,)),
+            dma((2, pieces)),
+            dma((2, pieces)),
         ],
         compiler_params=pltpu.CompilerParams(
             collective_id=0, has_side_effects=True, vmem_limit_bytes=52 * 2**20

time: 109 us -> 107 us (0.982)
  Pallas kernels: 103 us -> 101 us
    pallas_call x1, Pallas kernels: 103 us -> 101 us  [kernel_body(): pl.pallas_call(functools.partial(kernel, (n_dp, n_owner, cap, rank, parts...]
where the time goes in v4:
time: 107 us
  Pallas kernels  101 us (94%)
  local copies, waits for them, and re-layouts  2.56 us (2%)
  other arithmetic  2.14 us (2%)
    pallas_call x1, Pallas kernels, kernel_body(): pl.pallas_call(functools.partial(kernel, (n_dp, n_owner, cap, rank, parts...  101 us
    unnamed x14, local copies, waits for them, and re-layouts  2.56 us

profile of v4, /device:TPU:9, one launch (start us, length us, event | category | flops | bytes accessed | tf_op | source)
XLA Modules:
  0.0 106.6 jit_solution(2945403446780687124)
XLA Ops:
  0.6 0.0 copy-start
  0.6 0.9 copy-done
  1.6 0.0 copy-start.1
  1.6 0.9 copy-done.1
  2.5 0.0 copy-start.2
  2.5 0.7 copy-done.2
  3.2 0.0 copy-start.3
  3.2 0.0 copy-start.4
  3.2 0.0 copy-start.5
  3.2 0.0 copy-start.6
  3.2 101.2 %step.1 = (f32[64,2048]{1,0:T(8,128)S(1)}, f32[64,2048]{1,0:T(8,128)S(1)}, f32[1,128]{1,0:T(1,128)S(1)}) custom-call(s32[1,128]{1,0:T(1,128)S(1)} %bitcast.35, bf16[128,8192]{1,0:T(8,128)(2,1)} %tok_ref.1, bf16[128,8192]{1,0:T(8,128)(2,1)} %res_ref.1, bf16[64,2048]{1,0:T(8,128)(2,1)S(1)} %bitcast.33, bf16[64,2048]{1,0:T(8,128)(2,1)S(1)} %bitcast.34), custom_call_target="tpu_custom_call" | custom-call | tf_op jit(solution)/shard_map/step/pallas_call | solution.py:492
  104.4 0.0 copy-done.3
  104.4 0.0 copy-done.4
  104.5 0.0 copy-done.5
  104.5 0.0 copy-done.6
  104.5 1.6 %fusion.4 = (f32[1,64,2048]{2,1,0:T(8,128)}, f32[1,64,2048]{2,1,0:T(8,128)}) fusion(f32[64,2048]{1,0:T(8,128)S(1)} %get-tuple-element.6, bf16[1,64,2048]{2,1,0:T(8,128)(2,1)S(1)} %copy-done.3, bf16[1,64,2048]{2,1,0:T(8,128)(2,1)S(1)} %copy-done.4, f32[64,2048]{1,0:T(8,128)S(1)} %get-tuple-element.7, bf16[1,64,2048]{2,1,0:T(8,128)(2,1)S(1)} %copy-done.5, ...), kind=kLoop, calls=%fused_computation.6 | loop fusion | flops 2883584 | bytes 3145728 | tf_op jit(solution)/shard_map/div | solution.py:17
  106.1 0.5 multiply_bitcast_fusion
Async XLA Ops:
  0.6 1.0 copy-start
  1.6 0.9 copy-start.1
  2.5 0.7 copy-start.2
  3.2 101.2 %copy-start.3 = (bf16[1,64,2048]{2,1,0:T(8,128)(2,1)S(1)}, bf16[1,64,2048]{2,1,0:T(8,128)(2,1)}, u32[]{:S(2)}) copy-start(bf16[1,64,2048]{2,1,0:T(8,128)(2,1)} %param.15) | copy-start | bytes 786436
  3.2 101.3 %copy-start.4 = (bf16[1,64,2048]{2,1,0:T(8,128)(2,1)S(1)}, bf16[1,64,2048]{2,1,0:T(8,128)(2,1)}, u32[]{:S(2)}) copy-start(bf16[1,64,2048]{2,1,0:T(8,128)(2,1)} %param.14) | copy-start | bytes 786436
  3.2 101.3 %copy-start.5 = (bf16[1,64,2048]{2,1,0:T(8,128)(2,1)S(1)}, bf16[1,64,2048]{2,1,0:T(8,128)(2,1)}, u32[]{:S(2)}) copy-start(bf16[1,64,2048]{2,1,0:T(8,128)(2,1)} %param.17) | copy-start | bytes 786436
  3.2 101.3 %copy-start.6 = (bf16[1,64,2048]{2,1,0:T(8,128)(2,1)S(1)}, bf16[1,64,2048]{2,1,0:T(8,128)(2,1)}, u32[]{:S(2)}) copy-start(bf16[1,64,2048]{2,1,0:T(8,128)(2,1)} %param.16) | copy-start | bytes 786436
